TPU v7x, 128 devices: a whole 4x4x4 slice. The times are simulated.
128 devices in a mesh: dp: 8 (over x, core), tensor: 16 (over z, y).
Axes of the slice: x: 4, y: 4, z: 4, core: 2. Of those that a mesh axis runs over, the one named last changes fastest.
Arguments:
- tokens: bfloat16 [512, 8192], P(None, 'dp'), may hold values from -6 to 6
- gate_codes: int32 [8192, 32768], P('dp', 'tensor'), may hold values from 0 to 15
- up_codes: int32 [8192, 32768], P('dp', 'tensor'), may hold values from 0 to 15
- down_codes: int32 [32768, 8192], P('tensor', 'dp'), may hold values from 0 to 15
- gate_scale: int32 [32768], P('tensor'), may hold values from 8 to 39
- up_scale: int32 [32768], P('tensor'), may hold values from 8 to 39
- down_scale: int32 [8192], P('dp'), may hold values from 8 to 39
Outputs:
- mixed: bfloat16 [512, 8192], P('tensor', 'dp')
All inputs are finite; a program needn't handle non-finite values.
Results may differ from a plain program's by a relative error of at most 0.035.
Values may be sent and summed in bfloat16 or wider, within the bound.
A program may use at most 128 MiB of HBM per device.

v0:
```python
import math

import jax
import jax.numpy as jnp
from jax import lax
from jax.sharding import PartitionSpec as P

D = 8192
FF = 32768


def partner_2(value, axis, apart):
    mask = 2**apart
    pairs = [(source, source ^ mask) for source in range(lax.axis_size(axis))]
    return lax.ppermute(value, axis, pairs)


def sylvester(order_size, kind):
    hadamard = jnp.ones((1, 1), kind)
    while hadamard.shape[0] < order_size:
        top_rows = jnp.concatenate([hadamard, hadamard], axis=1)
        low_rows = jnp.concatenate([hadamard, -hadamard], axis=1)
        hadamard = jnp.concatenate([top_rows, low_rows], axis=0)
    return hadamard


def body(tokens, gate_codes, up_codes, down_codes, gate_scale, up_scale, down_scale):
    shard_units = gate_codes.shape[1]
    paired = jnp.concatenate(
        [(gate_codes - 8).astype(jnp.bfloat16), (up_codes - 8).astype(jnp.bfloat16)], axis=1
    )
    down_matrix = (down_codes - 8).astype(jnp.bfloat16)
    summed = lax.psum_scatter(
        jnp.dot(tokens, paired, preferred_element_type=jnp.float32).astype(jnp.bfloat16),
        "dp",
        scatter_dimension=0,
        tiled=True,
    ).astype(jnp.float32)
    gate_part = summed[:, :shard_units] * (gate_scale.astype(jnp.float32) / (128.0 * math.sqrt(D)))
    up_part = summed[:, shard_units:] * (up_scale.astype(jnp.float32) / (128.0 * math.sqrt(D)))
    hidden = (jax.nn.silu(gate_part) * up_part).astype(jnp.bfloat16)
    rotated_part = jnp.dot(
        hidden, sylvester(shard_units, jnp.bfloat16), preferred_element_type=jnp.float32
    )
    index_here = lax.axis_index("tensor")
    levels = lax.axis_size("tensor").bit_length() - 1
    for position in range(levels):
        partner = partner_2(rotated_part.astype(jnp.bfloat16), "tensor", position).astype(
            rotated_part.dtype
        )
        upper_half = jnp.bitwise_and(jnp.right_shift(index_here, position), 1) == 1
        rotated_part = jnp.where(upper_half, partner - rotated_part, rotated_part + partner)
    rotated = (rotated_part / math.sqrt(FF)).astype(jnp.bfloat16)
    partial_value = jnp.dot(
        lax.all_gather(rotated, "dp", axis=0, tiled=True),
        down_matrix,
        preferred_element_type=jnp.float32,
    )
    summed_out = lax.psum_scatter(
        partial_value.astype(jnp.bfloat16), "tensor", scatter_dimension=0, tiled=True
    ).astype(jnp.float32)
    return (summed_out * (down_scale.astype(jnp.float32) / (64.0 * math.sqrt(FF)))).astype(
        jnp.bfloat16
    )


def solution(mesh):
    in_specs = (
        P(None, "dp"),
        P("dp", "tensor"),
        P("dp", "tensor"),
        P("tensor", "dp"),
        P("tensor"),
        P("tensor"),
        P("dp"),
    )
    out_specs = P("tensor", "dp")
    return jax.shard_map(body, mesh=mesh, in_specs=in_specs, out_specs=out_specs, check_vma=False)
```

profile of v0, /device:TPU:1, one launch (start us, length us, event | category | flops | bytes accessed | tf_op | source)
XLA Modules:
  0.0 229.3 jit_solution(7822840753005459859)
XLA Ops:
  6.5 0.0 copy-start
  6.5 0.0 reduce-scatter.7.cloned.1.call-start
  6.5 11.7 %add_convert_fusion.1 = (bf16[1024,2048]{1,0:T(8,128)(2,1)}, bf16[1024,2048]{1,0:T(8,128)(2,1)}) fusion(s32[1024,2048]{1,0:T(8,128)} %param.9, s32[1024,2048]{1,0:T(8,128)} %param.8), kind=kLoop, calls=%fused_computation.5 | loop fusion | flops 8388608 | bytes 25165824 | tf_op jit(solution)/shard_map/convert_element_type | solution.py:30
  18.2 0.0 copy-done
  18.2 10.0 %fusion.7 = bf16[512,4096]{0,1:T(8,128)(2,1)} fusion(bf16[512,1024]{1,0:T(8,128)(2,1)S(1)} %copy-done, bf16[1024,2048]{1,0:T(8,128)(2,1)} %get-tuple-element.9, bf16[1024,2048]{1,0:T(8,128)(2,1)} %get-tuple-element.10), kind=kOutput, calls=%fused_computation.8 | convolution fusion | flops 4313841664 | bytes 13631488 | tf_op jit(solution)/shard_map/dot_general | solution.py:34
  28.2 0.0 copy-start.1
  28.2 0.0 copy-start.2
  28.2 6.5 %copy.8 = bf16[512,4096]{1,0:T(8,128)(2,1)} copy(bf16[512,4096]{0,1:T(8,128)(2,1)} %fusion.7) | data formatting | bytes 8388608
  34.7 0.0 reduce-scatter.7.cloned.1.call-update
  34.8 0.0 all-gather.2.cloned.1.call-start
  34.8 0.0 copy-done.1
  34.8 0.0 copy-done.2
  34.9 38.1 %reduce-scatter.7.cloned.1.call-done = bf16[64,4096]{1,0:T(8,128)(2,1)} async-done(((bf16[512,4096]{1,0:T(8,128)(2,1)}), bf16[64,4096]{1,0:T(8,128)(2,1)}) %reduce-scatter.7.cloned.1.call-update) | async-done | bytes 524304
  73.0 1.5 copy.9
  74.5 0.1 convert_element_type.70
  74.6 4.6 %fusion.30 = (bf16[64,2048]{1,0:T(8,128)(2,1)S(1)}, f32[64,2048]{1,0:T(8,128)S(1)}) fusion(bf16[2048,2048]{1,0:T(8,128)(2,1)} %constant.42.clone.1, f32[64,4096]{0,1:T(8,128)S(1)} %convert_element_type.70, f32[2048]{0:T(1024)S(1)} %get-tuple-element.11, f32[2048]{0:T(1024)S(1)} %get-tuple-element.12), kind=kOutput, calls=%fused_computation.41 | convolution fusion | flops 538050560 | bytes 10240000 | tf_op jit(solution)/shard_map/dot_general | solution.py:42
  79.2 1.3 collective-permute-start
  80.5 4.0 %collective-permute-done = bf16[64,2048]{1,0:T(8,128)(2,1)S(1)} collective-permute-done((bf16[64,2048]{1,0:T(8,128)(2,1)S(1)}, bf16[64,2048]{1,0:T(8,128)(2,1)S(1)}, u32[]{:S(2)}, u32[]{:S(2)}) %collective-permute-start) | collective-permute-done | bytes 262176 | tf_op jit(solution)/shard_map/ppermute | solution.py:15
  84.5 0.1 fusion.24
  84.6 2.8 %collective-permute-start.1 = (bf16[64,2048]{1,0:T(8,128)(2,1)S(1)}, bf16[64,2048]{1,0:T(8,128)(2,1)S(1)}, u32[]{:S(2)}, u32[]{:S(2)}) collective-permute-start(bf16[64,2048]{1,0:T(8,128)(2,1)S(1)} %fusion.24), channel_id=1, source_target_pairs={{0,2},{1,3},{2,0},{3,1},{4,6},{5,7},{6,4},{7,5},{8,10},{9,11},{10,... | collective-permute-start | bytes 786440 | tf_op jit(solution)/shard_map/ppermute | solution.py:15
  87.4 6.3 %collective-permute-done.1 = bf16[64,2048]{1,0:T(8,128)(2,1)S(1)} collective-permute-done((bf16[64,2048]{1,0:T(8,128)(2,1)S(1)}, bf16[64,2048]{1,0:T(8,128)(2,1)S(1)}, u32[]{:S(2)}, u32[]{:S(2)}) %collective-permute-start.1) | collective-permute-done | bytes 262176 | tf_op jit(solution)/shard_map/ppermute | solution.py:15
  93.7 0.1 fusion.28
  93.8 1.4 collective-permute-start.2
  95.2 3.9 %collective-permute-done.2 = bf16[64,2048]{1,0:T(8,128)(2,1)S(1)} collective-permute-done((bf16[64,2048]{1,0:T(8,128)(2,1)S(1)}, bf16[64,2048]{1,0:T(8,128)(2,1)S(1)}, u32[]{:S(2)}, u32[]{:S(2)}) %collective-permute-start.2) | collective-permute-done | bytes 262176 | tf_op jit(solution)/shard_map/ppermute | solution.py:15
  99.1 0.1 fusion.23
  99.2 3.0 %collective-permute-start.3 = (bf16[64,2048]{1,0:T(8,128)(2,1)S(1)}, bf16[64,2048]{1,0:T(8,128)(2,1)S(1)}, u32[]{:S(2)}, u32[]{:S(2)}) collective-permute-start(bf16[64,2048]{1,0:T(8,128)(2,1)S(1)} %fusion.23), channel_id=1, source_target_pairs={{0,8},{1,9},{2,10},{3,11},{4,12},{5,13},{6,14},{7,15},{8,0},{9,1},... | collective-permute-start | bytes 786440 | tf_op jit(solution)/shard_map/ppermute | solution.py:15
  102.2 6.4 %collective-permute-done.3 = bf16[64,2048]{1,0:T(8,128)(2,1)S(1)} collective-permute-done((bf16[64,2048]{1,0:T(8,128)(2,1)S(1)}, bf16[64,2048]{1,0:T(8,128)(2,1)S(1)}, u32[]{:S(2)}, u32[]{:S(2)}) %collective-permute-start.3) | collective-permute-done | bytes 262176 | tf_op jit(solution)/shard_map/ppermute | solution.py:15
  108.6 0.9 fusion.20
  109.5 0.0 copy-start.3
  109.5 0.0 all-gather.2.cloned.1.call-update
  109.5 0.0 reduce-scatter.5.cloned.1.call-start
  109.5 32.7 %all-gather.2.cloned.1.call-done = bf16[512,2048]{1,0:T(8,128)(2,1)} async-done(((bf16[64,2048]{1,0:T(8,128)(2,1)}), bf16[512,2048]{1,0:T(8,128)(2,1)}) %all-gather.2.cloned.1.call-update) | async-done | bytes 2097168 | tf_op jit(solution)/shard_map/all_gather | solution.py:55
  142.3 7.3 %fusion.12 = bf16[512,1024]{1,0:T(8,128)(2,1)} fusion(bf16[512,2048]{1,0:T(8,128)(2,1)} %all-gather.2.cloned.1.call-done, s32[2048,1024]{1,0:T(8,128)} %param.10), kind=kOutput, calls=%fused_computation.11 | convolution fusion | flops 2152202240 | bytes 11534336 | tf_op jit(solution)/shard_map/dot_general | solution.py:54
  149.6 0.0 reduce-scatter.5.cloned.1.call-update
  149.6 0.0 copy-done.3
  149.7 71.6 %reduce-scatter.5.cloned.1.call-done = bf16[32,1024]{1,0:T(8,128)(2,1)} async-done(((bf16[512,1024]{1,0:T(8,128)(2,1)}), bf16[32,1024]{1,0:T(8,128)(2,1)}) %reduce-scatter.5.cloned.1.call-update) | async-done | bytes 65552 | tf_op jit(solution)/shard_map/reduce_scatter | solution.py:59
  221.2 1.5 multiply_convert_fusion
  (2 shorter events, 0.0 us)
Async XLA Ops:
  6.5 11.7 %copy-start = (bf16[512,1024]{1,0:T(8,128)(2,1)S(1)}, bf16[512,1024]{1,0:T(8,128)(2,1)}, u32[]{:S(2)}) copy-start(bf16[512,1024]{1,0:T(8,128)(2,1)} %param.7) | copy-start | bytes 3145732
  6.5 66.4 %reduce-scatter.7.cloned.1.call-start = ((), (), s32[]{:S(2)}) async-start(), calls=%async_computation.4 | async-start | bytes 4718592
  28.2 6.6 %copy-start.1 = (s32[2048]{0:T(1024)S(1)}, s32[2048]{0:T(1024)}, u32[]{:S(2)}) copy-start(s32[2048]{0:T(1024)} %param.12) | copy-start | bytes 24580
  28.2 6.6 %copy-start.2 = (s32[2048]{0:T(1024)S(1)}, s32[2048]{0:T(1024)}, u32[]{:S(2)}) copy-start(s32[2048]{0:T(1024)} %param.11) | copy-start | bytes 24580
  34.8 107.5 %all-gather.2.cloned.1.call-start = ((), (), s32[]{:S(2)}) async-start(), calls=%async_computation.2 | async-start | bytes 2359296 | tf_op jit(solution)/shard_map/all_gather | solution.py:55
  79.2 5.3 %collective-permute-start = (bf16[64,2048]{1,0:T(8,128)(2,1)S(1)}, bf16[64,2048]{1,0:T(8,128)(2,1)S(1)}, u32[]{:S(2)}, u32[]{:S(2)}) collective-permute-start(bf16[64,2048]{1,0:T(8,128)(2,1)S(1)} %get-tuple-element.7), channel_id=1, source_target_pairs={{0,1},{1,0},{2,3},{3,2},{4,5},{5,4},{6,7},{7,6},{8,9},{9,8},{10,11... | collective-permute-start | bytes 786440 | tf_op jit(solution)/shard_map/ppermute | solution.py:15
  84.6 9.1 %collective-permute-start.1 = (bf16[64,2048]{1,0:T(8,128)(2,1)S(1)}, bf16[64,2048]{1,0:T(8,128)(2,1)S(1)}, u32[]{:S(2)}, u32[]{:S(2)}) collective-permute-start(bf16[64,2048]{1,0:T(8,128)(2,1)S(1)} %fusion.24), channel_id=1, source_target_pairs={{0,2},{1,3},{2,0},{3,1},{4,6},{5,7},{6,4},{7,5},{8,10},{9,11},{10,... | collective-permute-start | bytes 786440 | tf_op jit(solution)/shard_map/ppermute | solution.py:15
  93.8 5.3 %collective-permute-start.2 = (bf16[64,2048]{1,0:T(8,128)(2,1)S(1)}, bf16[64,2048]{1,0:T(8,128)(2,1)S(1)}, u32[]{:S(2)}, u32[]{:S(2)}) collective-permute-start(bf16[64,2048]{1,0:T(8,128)(2,1)S(1)} %get-tuple-element.5), channel_id=1, source_target_pairs={{0,4},{1,5},{2,6},{3,7},{4,0},{5,1},{6,2},{7,3},{8,12},{9,13},{10,... | collective-permute-start | bytes 786440 | tf_op jit(solution)/shard_map/ppermute | solution.py:15
  99.2 9.4 %collective-permute-start.3 = (bf16[64,2048]{1,0:T(8,128)(2,1)S(1)}, bf16[64,2048]{1,0:T(8,128)(2,1)S(1)}, u32[]{:S(2)}, u32[]{:S(2)}) collective-permute-start(bf16[64,2048]{1,0:T(8,128)(2,1)S(1)} %fusion.23), channel_id=1, source_target_pairs={{0,8},{1,9},{2,10},{3,11},{4,12},{5,13},{6,14},{7,15},{8,0},{9,1},... | collective-permute-start | bytes 786440 | tf_op jit(solution)/shard_map/ppermute | solution.py:15
  109.5 40.2 %copy-start.3 = (s32[1024]{0:T(1024)S(1)}, s32[1024]{0:T(1024)}, u32[]{:S(2)}) copy-start(s32[1024]{0:T(1024)} %param.13) | copy-start | bytes 12292
  109.5 111.7 %reduce-scatter.5.cloned.1.call-start = ((), (), s32[]{:S(2)}) async-start(), calls=%async_computation.3 | async-start | bytes 1114112 | tf_op jit(solution)/shard_map/reduce_scatter | solution.py:59
Sparse Core Ops, SparseCore 0:
  34.9 38.0 reduce-scatter.6
  109.6 32.6 all-gather.1
  149.8 71.4 reduce-scatter.4
where the time goes:
time: 230 us; the launch traced here: 229 us
  waiting for transfers between devices  163 us (71%)
  matrix products  21.9 us (10%)
  other arithmetic  14.5 us (6%)
  between operations  13.2 us (6%)
  starting transfers between devices  8.56 us (4%)
  local copies, waits for them, and re-layouts  8.05 us (4%)
    reduce_scatter x1, waiting for transfers between devices, body(): lax.psum_scatter(partial_value.astype(jnp.bfloat16), 'tensor', scatter_di...  71.6 us
    unnamed x4, waiting for transfers between devices  38.2 us
    all_gather x1, waiting for transfers between devices, body(): lax.all_gather(rotated, 'dp', axis=0, tiled=True)  32.7 us
    ppermute x4, waiting for transfers between devices, partner_2(): return lax.ppermute(value, axis, pairs)  20.6 us
    convert_element_type x1, other arithmetic, body(): (up_codes - 8).astype(jnp.bfloat16)  11.7 us
    dot_general x1, matrix products, body(): jnp.dot(tokens, paired, preferred_element_type=jnp.float32)  10 us
    ppermute x4, starting transfers between devices, partner_2(): return lax.ppermute(value, axis, pairs)  8.47 us
    unnamed x10, local copies, waits for them, and re-layouts  8.05 us
  transfers between devices with their start and end apart: 7, of which 7 were waited for; matrix products, arithmetic and copies ran while one was open for 0% of the time, Pallas kernels for 0%

commit v1 on v0

v1 whole, which is shorter than its diff:
```python
import functools
import math

import jax
import jax.numpy as jnp
from jax import lax
from jax.experimental import pallas as pl
from jax.experimental.pallas import tpu as pltpu
from jax.sharding import PartitionSpec as P

D = 8192
FF = 32768
TOKENS = 512
NX = 4
OWN = TOKENS // (2 * NX)
SUB = OWN // 2
TILES = 8
LAG_B, LAG_C, LAG_D = 1, 2, 3
MESH = pl.DeviceIdType.MESH
F32 = jnp.float32
BF16 = jnp.bfloat16


def remote(src, dst, send_sem, recv_sem, device):
    return pltpu.make_async_remote_copy(
        src_ref=src,
        dst_ref=dst,
        send_sem=send_sem,
        recv_sem=recv_sem,
        device_id=device,
        device_id_type=MESH,
    )


def walsh(parts):
    stride = 1
    while stride < len(parts):
        done = list(parts)
        for i in range(len(parts)):
            if i & stride == 0:
                done[i] = parts[i] + parts[i + stride]
                done[i + stride] = parts[i] - parts[i + stride]
        parts = done
        stride *= 2
    return parts


def signs(size):
    rows = lax.broadcasted_iota(jnp.int32, (size, size), 0)
    cols = lax.broadcasted_iota(jnp.int32, (size, size), 1)
    bits = jnp.bitwise_and(rows, cols)
    for shift in (8, 4, 2, 1):
        bits = jnp.bitwise_xor(bits, jnp.right_shift(bits, shift))
    return (1 - 2 * jnp.bitwise_and(bits, 1)).astype(F32).astype(BF16)


def kernel(
    nt, ff,
    tok_hbm, gate_hbm, up_hbm, down_hbm, gs_ref, us_ref, ds_ref,
    out_ref,
    tok_in, tok, codes, down_codes, w, wd, had,
    core_out, core_in, acc, x_out, x_in,
    rot, z, a, r, y, part, gathered,
    tok_sem, code_sem, down_sem,
    core_ssem, core_rsem, x_ssem, x_rsem,
    z_ssem, z_rsem, r_ssem, r_rsem, ag_ssem, ag_rsem, rs_ssem, rs_rsem,
):
    dp = lax.axis_index("dp")
    me = lax.axis_index("tensor")
    x = dp // 2
    c = dp % 2
    right = lax.rem(x + 1, NX)
    left = lax.rem(x + NX - 1, NX)
    across = lax.rem(x + 2, NX)
    dev_core = (x * 2 + 1 - c, me)
    dev_right = (right * 2 + c, me)
    dev_left = (left * 2 + c, me)
    units = gate_hbm.shape[1]
    wide = units // TILES
    depth = gate_hbm.shape[0]
    d_rows = down_hbm.shape[0] // TILES
    group = TOKENS // (NX * nt)
    piece = units // nt

    def peer(k):
        return lax.rem(me + k, nt)

    barrier = pltpu.get_barrier_semaphore()
    for device in (dev_core, dev_right, dev_left):
        pl.semaphore_signal(barrier, inc=1, device_id=device, device_id_type=MESH)

    def greet(k, carry):
        pl.semaphore_signal(barrier, inc=1, device_id=(dp, peer(k)), device_id_type=MESH)
        return carry

    lax.fori_loop(1, nt, greet, 0)

    tok_copy = pltpu.make_async_copy(tok_hbm, tok_in, tok_sem.at[0])
    tok_copy.start()

    def gate_copy(t):
        return pltpu.make_async_copy(
            gate_hbm.at[:, pl.ds(pl.multiple_of(t * wide, wide), wide)], codes.at[t, 0], code_sem.at[t, 0]
        )

    def up_copy(t):
        return pltpu.make_async_copy(
            up_hbm.at[:, pl.ds(pl.multiple_of(t * wide, wide), wide)], codes.at[t, 1], code_sem.at[t, 1]
        )

    def down_copy(t):
        rows = pl.ds(pl.multiple_of(t * d_rows, d_rows), d_rows)
        return pltpu.make_async_copy(down_hbm.at[rows, :], down_codes.at[rows, :], down_sem.at[t])

    def start_codes(t, carry):
        gate_copy(t).start()
        up_copy(t).start()
        return carry

    def start_down(t, carry):
        down_copy(t).start()
        return carry

    lax.fori_loop(0, TILES, start_codes, 0)
    lax.fori_loop(0, TILES, start_down, 0)

    had[...] = signs(wide)

    tok_copy.wait()
    half_groups = nt // 2
    for half in range(2):
        for chip in range(NX):
            rows = []
            for j in range(half_groups):
                first = (half * half_groups + j) * (TOKENS // nt) + chip * group
                rows.append(tok_in[first // 16 * 16 : first // 16 * 16 + max(16, group), :].astype(F32)[
                    first % 16 : first % 16 + group])
            start = half * (TOKENS // 2) + chip * OWN
            tok[start : start + OWN, :] = jnp.concatenate(rows, axis=0).astype(BF16)

    other_rows = pl.ds(pl.multiple_of((1 - c) * (TOKENS // 2), TOKENS // 2), TOKENS // 2)
    own_rows = pl.ds(pl.multiple_of(c * (TOKENS // 2), TOKENS // 2), TOKENS // 2)

    def rows_of(chip, half):
        return pl.ds(pl.multiple_of(chip * OWN + half * SUB, SUB), SUB)

    def core_copy(t):
        return remote(core_out.at[t], core_in.at[t], core_ssem.at[t], core_rsem.at[t], dev_core)

    def x_copy(t, way, kind):
        return remote(
            x_out.at[t, way, kind], x_in.at[t, way, kind], x_ssem.at[t, way, kind], x_rsem.at[t, way, kind],
            dev_right if way == 0 else dev_left,
        )

    def stage_a(t):
        gate_copy(t).wait()
        up_copy(t).wait()
        w[:, :wide] = (codes[t, 0] - 8).astype(F32).astype(BF16)
        w[:, wide:] = (codes[t, 1] - 8).astype(F32).astype(BF16)
        core_out[t] = jnp.dot(tok[other_rows, :], w[...], preferred_element_type=F32).astype(BF16)

        @pl.when(t == 0)
        def _():
            pl.semaphore_wait(barrier, 3 + nt - 1)

        core_copy(t).start()
        acc[t] = jnp.dot(tok[own_rows, :], w[...], preferred_element_type=F32)
        down_copy(t).wait()
        rows = pl.ds(pl.multiple_of(t * d_rows, d_rows), d_rows)
        wd[rows, :] = (down_codes[rows, :] - 8).astype(F32).astype(BF16)

    def stage_b(t):
        core_copy(t).wait_recv()

        def both(rows):
            return acc[t, rows, :] + core_in[t, rows, :].astype(F32)

        x_out[t, 0, 0] = both(rows_of(across, 0)).astype(BF16)
        x_copy(t, 0, 0).start()
        x_out[t, 1, 0] = both(rows_of(across, 1)).astype(BF16)
        x_copy(t, 1, 0).start()
        x_out[t, 0, 1] = both(rows_of(right, 1)).astype(BF16)
        x_copy(t, 0, 1).start()
        x_out[t, 1, 1] = both(rows_of(left, 0)).astype(BF16)
        x_copy(t, 1, 1).start()
        for rows in (rows_of(right, 0), rows_of(left, 1), rows_of(x, 0), rows_of(x, 1)):
            acc[t, rows, :] = both(rows)

    def stage_c(t):
        x_copy(t, 0, 0).wait_recv()
        x_out[t, 0, 2] = (acc[t, rows_of(right, 0), :] + x_in[t, 0, 0].astype(F32)).astype(BF16)
        x_copy(t, 0, 2).start()
        x_copy(t, 1, 0).wait_recv()
        x_out[t, 1, 2] = (acc[t, rows_of(left, 1), :] + x_in[t, 1, 0].astype(F32)).astype(BF16)
        x_copy(t, 1, 2).start()

    def stage_d(t):
        for way in range(2):
            for kind in (1, 2):
                x_copy(t, way, kind).wait_recv()
        low = acc[t, rows_of(x, 0), :] + x_in[t, 0, 2].astype(F32) + x_in[t, 1, 1].astype(F32)
        high = acc[t, rows_of(x, 1), :] + x_in[t, 0, 1].astype(F32) + x_in[t, 1, 2].astype(F32)
        total = jnp.concatenate([low, high], axis=0)
        unit = 1.0 / (128.0 * math.sqrt(D))
        gate = total[:, :wide] * (gs_ref[t].astype(F32) * unit)
        up = total[:, wide:] * (us_ref[t].astype(F32) * unit)
        hidden = (gate / (1.0 + jnp.exp(-gate)) * up).astype(BF16)
        rot[t] = jnp.dot(hidden, had[...], preferred_element_type=F32)

    def step(s, carry):
        pl.when(s < TILES)(lambda: stage_a(s))
        pl.when(jnp.logical_and(s >= LAG_B, s < TILES + LAG_B))(lambda: stage_b(s - LAG_B))
        pl.when(jnp.logical_and(s >= LAG_C, s < TILES + LAG_C))(lambda: stage_c(s - LAG_C))
        pl.when(s >= LAG_D)(lambda: stage_d(s - LAG_D))
        return carry

    lax.fori_loop(0, TILES + LAG_D, step, 0)

    for rows in range(0, OWN, 16):
        mixed = walsh([rot[t, rows : rows + 16, :] for t in range(TILES)])
        flat = jnp.concatenate(mixed, axis=1).astype(BF16)
        for j in range(nt):
            z[j, rows : rows + 16, :] = flat[:, j * piece : (j + 1) * piece]

    def z_copy(j, slot):
        return remote(z.at[j], a.at[slot], z_ssem.at[j], z_rsem.at[slot], (dp, j))

    def z_send(k, carry):
        z_copy(peer(k), me).start()
        return carry

    def z_wait(k, carry):
        z_copy(me, peer(k)).wait_recv()
        return carry

    lax.fori_loop(1, nt, z_send, 0)
    a[me] = z[me]
    lax.fori_loop(1, nt, z_wait, 0)

    for rows in range(0, OWN, 16):
        mixed = walsh([a[i, rows : rows + 16, :].astype(F32) for i in range(nt)])
        for j in range(nt):
            r[j, rows : rows + 16, :] = (mixed[j] * (1.0 / math.sqrt(ff))).astype(BF16)

    my_rows = pl.ds(pl.multiple_of(c * OWN, OWN), OWN)
    other_core = pl.ds(pl.multiple_of((1 - c) * OWN, OWN), OWN)

    def r_copy(j, slot):
        cols = pl.ds(pl.multiple_of(slot * piece, piece), piece)
        return remote(r.at[j], y.at[x, my_rows, cols], r_ssem.at[j], r_rsem.at[slot], (dp, j))

    def r_send(k, carry):
        r_copy(peer(k), me).start()
        return carry

    def r_wait(k, carry):
        r_copy(me, peer(k)).wait_recv()
        return carry

    lax.fori_loop(1, nt, r_send, 0)
    y[x, my_rows, pl.ds(pl.multiple_of(me * piece, piece), piece)] = r[me]
    lax.fori_loop(1, nt, r_wait, 0)

    half_rows = [pl.ds(pl.multiple_of(c * OWN + h * SUB, SUB), SUB) for h in range(2)]

    def ag(sem, chip, rows, device):
        return remote(y.at[chip, rows, :], y.at[chip, rows, :], ag_ssem.at[sem], ag_rsem.at[sem], device)

    ag(0, x, my_rows, dev_right).start()
    ag(1, x, my_rows, dev_left).start()
    ag(2, x, my_rows, dev_core).start()

    def rs_copy(chip, j, slot):
        return remote(
            part.at[chip, j], gathered.at[chip, slot], rs_ssem.at[chip, j], rs_rsem.at[chip, slot], (dp, j)
        )

    def down(chip):
        result = jnp.dot(y[chip], wd[...], preferred_element_type=F32)
        middle = result.shape[1] // 2
        for j in range(nt):
            rows = result[j * group : (j + 1) * group]
            part[chip, j] = jnp.concatenate([rows[:, :middle], rows[:, middle:]], axis=0).astype(BF16)

        def send(k, carry):
            rs_copy(chip, peer(k), me).start()
            return carry

        lax.fori_loop(1, nt, send, 0)
        gathered[chip, me] = part[chip, me]

    ag(2, x, other_core, dev_core).wait_recv()
    down(x)

    ag(0, left, my_rows, dev_right).wait_recv()
    ag(3, left, half_rows[0], dev_right).start()
    ag(4, left, my_rows, dev_core).start()
    ag(1, right, my_rows, dev_left).wait_recv()
    ag(5, right, half_rows[1], dev_left).start()
    ag(6, right, my_rows, dev_core).start()

    ag(4, left, other_core, dev_core).wait_recv()
    down(left)
    ag(6, right, other_core, dev_core).wait_recv()
    down(right)

    ag(3, across, half_rows[0], dev_right).wait_recv()
    ag(7, across, half_rows[0], dev_core).start()
    ag(5, across, half_rows[1], dev_left).wait_recv()
    ag(8, across, half_rows[1], dev_core).start()
    other_half = [pl.ds(pl.multiple_of((1 - c) * OWN + h * SUB, SUB), SUB) for h in range(2)]
    ag(7, across, other_half[0], dev_core).wait_recv()
    ag(8, across, other_half[1], dev_core).wait_recv()
    down(across)

    def rs_wait(n, carry):
        rs_copy(n // (nt - 1), me, peer(n % (nt - 1) + 1)).wait_recv()
        return carry

    lax.fori_loop(0, NX * (nt - 1), rs_wait, 0)
    scale = ds_ref[...].astype(F32) * (1.0 / (64.0 * math.sqrt(ff)))
    blocks = []
    for chip in range(NX):
        total = gathered[chip, 0].astype(F32)
        for i in range(1, nt):
            total = total + gathered[chip, i].astype(F32)
        blocks.append(jnp.concatenate([total[:group], total[group:]], axis=1) * scale)
    out_ref[...] = jnp.concatenate(blocks, axis=0).astype(BF16)

    def core_done(t, carry):
        core_copy(t).wait_send()
        for way in range(2):
            for kind in range(3):
                x_copy(t, way, kind).wait_send()
        return carry

    lax.fori_loop(0, TILES, core_done, 0)

    def peers_done(k, carry):
        z_copy(peer(k), me).wait_send()
        r_copy(peer(k), me).wait_send()
        return carry

    lax.fori_loop(1, nt, peers_done, 0)

    def rs_done(n, carry):
        rs_copy(n // (nt - 1), peer(n % (nt - 1) + 1), me).wait_send()
        return carry

    lax.fori_loop(0, NX * (nt - 1), rs_done, 0)
    ag(0, x, my_rows, dev_right).wait_send()
    ag(1, x, my_rows, dev_left).wait_send()
    ag(2, x, my_rows, dev_core).wait_send()
    ag(3, left, half_rows[0], dev_right).wait_send()
    ag(4, left, my_rows, dev_core).wait_send()
    ag(5, right, half_rows[1], dev_left).wait_send()
    ag(6, right, my_rows, dev_core).wait_send()
    ag(7, across, half_rows[0], dev_core).wait_send()
    ag(8, across, half_rows[1], dev_core).wait_send()


def body(tokens, gate_codes, up_codes, down_codes, gate_scale, up_scale, down_scale):
    nt = lax.axis_size("tensor")
    depth, units = gate_codes.shape
    width = down_codes.shape[1]
    wide = units // TILES
    piece = units // nt
    group = TOKENS // (NX * nt)
    dma = pltpu.SemaphoreType.DMA
    any_space = pl.BlockSpec(memory_space=pl.ANY)
    vmem = pl.BlockSpec(memory_space=pltpu.VMEM)
    return pl.pallas_call(
        functools.partial(kernel, nt, units * nt),
        out_shape=jax.ShapeDtypeStruct((TOKENS // nt, width), BF16),
        in_specs=[any_space] * 4 + [vmem] * 3,
        out_specs=vmem,
        scratch_shapes=[
            pltpu.VMEM((TOKENS, depth), BF16),
            pltpu.VMEM((TOKENS, depth), BF16),
            pltpu.VMEM((TILES, 2, depth, wide), jnp.int32),
            pltpu.VMEM((units, width), jnp.int32),
            pltpu.VMEM((depth, 2 * wide), BF16),
            pltpu.VMEM((units, width), BF16),
            pltpu.VMEM((wide, wide), BF16),
            pltpu.VMEM((TILES, TOKENS // 2, 2 * wide), BF16),
            pltpu.VMEM((TILES, TOKENS // 2, 2 * wide), BF16),
            pltpu.VMEM((TILES, TOKENS // 2, 2 * wide), F32),
            pltpu.VMEM((TILES, 2, 3, SUB, 2 * wide), BF16),
            pltpu.VMEM((TILES, 2, 3, SUB, 2 * wide), BF16),
            pltpu.VMEM((TILES, OWN, wide), F32),
            pltpu.VMEM((nt, OWN, piece), BF16),
            pltpu.VMEM((nt, OWN, piece), BF16),
            pltpu.VMEM((nt, OWN, piece), BF16),
            pltpu.VMEM((NX, 2 * OWN, units), BF16),
            pltpu.VMEM((NX, nt, 2 * group, width // 2), BF16),
            pltpu.VMEM((NX, nt, 2 * group, width // 2), BF16),
            dma((1,)),
            dma((TILES, 2)),
            dma((TILES,)),
            dma((TILES,)),
            dma((TILES,)),
            dma((TILES, 2, 3)),
            dma((TILES, 2, 3)),
            dma((nt,)),
            dma((nt,)),
            dma((nt,)),
            dma((nt,)),
            dma((9,)),
            dma((9,)),
            dma((NX, nt)),
            dma((NX, nt)),
        ],
        compiler_params=pltpu.CompilerParams(
            collective_id=0, has_side_effects=True, vmem_limit_bytes=56 * 1024 * 1024
        ),
        cost_estimate=pl.CostEstimate(
            flops=2 * TOKENS * depth * 3 * units, bytes_accessed=12 * depth * units, transcendentals=OWN * units
        ),
    )(
        tokens, gate_codes, up_codes, down_codes,
        gate_scale.reshape(TILES, 1, wide), up_scale.reshape(TILES, 1, wide), down_scale.reshape(1, width),
    )


def solution(mesh):
    in_specs = (
        P(None, "dp"),
        P("dp", "tensor"),
        P("dp", "tensor"),
        P("tensor", "dp"),
        P("tensor"),
        P("tensor"),
        P("dp"),
    )
    return jax.shard_map(body, mesh=mesh, in_specs=in_specs, out_specs=P("tensor", "dp"), check_vma=False)
```

time: 230 us -> 79.7 us (0.35)
  waiting for transfers between devices: 163 us -> 0 us
  Pallas kernels: 0 us -> 78 us
  matrix products: 21.9 us -> 0 us
  other arithmetic: 14.5 us -> 0 us
  between operations: 13.2 us -> 0.01 us
  starting transfers between devices: 8.56 us -> 0 us
  local copies, waits for them, and re-layouts: 8.05 us -> 1.47 us
    pallas_call x0 -> x1, Pallas kernels: none -> 78 us  [body(): pl.pallas_call(functools.partial(kernel, nt, units * nt), out_shape=jax.S...]
    reduce_scatter x1 -> x0, waiting for transfers between devices: 71.6 us -> none  [body(): lax.psum_scatter(partial_value.astype(jnp.bfloat16), 'tensor', scatter_di...]
    unnamed x4 -> x0, waiting for transfers between devices: 38.2 us -> none
    all_gather x1 -> x0, waiting for transfers between devices: 32.7 us -> none  [body(): lax.all_gather(rotated, 'dp', axis=0, tiled=True)]
    dot_general x3 -> x0, matrix products: 21.9 us -> none  [the longest x1 10 us: body(): jnp.dot(tokens, paired, preferred_element_type=jnp.float32)]
    ppermute x4 -> x0, waiting for transfers between devices: 20.6 us -> none  [partner_2(): return lax.ppermute(value, axis, pairs)]
    convert_element_type x7 -> x0, other arithmetic: 14.5 us -> none  [the longest x1 11.7 us: body(): (up_codes - 8).astype(jnp.bfloat16)]
    ppermute x4 -> x0, starting transfers between devices: 8.47 us -> none  [partner_2(): return lax.ppermute(value, axis, pairs)]
  transfers between devices with their start and end apart: 7 -> 0, of which waited for: 7 -> 0; matrix products, arithmetic and copies ran while one was open for 0% -> 0% of each run, Pallas kernels for 0% -> 0%
where the time goes in v1:
time: 79.7 us; the launch traced here: 79.5 us
  Pallas kernels  78 us (98%)
  local copies, waits for them, and re-layouts  1.47 us (2%)
    pallas_call x1, Pallas kernels, body(): pl.pallas_call(functools.partial(kernel, nt, units * nt), out_shape=jax.S...  78 us

profile of v1, /device:TPU:1, one launch (start us, length us, event | category | flops | bytes accessed | tf_op | source)
XLA Modules:
  0.0 79.5 jit_solution(15232145164566268943)
XLA Ops:
  0.0 78.0 %shard_map.73 = bf16[32,1024]{1,0:T(8,128)(2,1)} custom-call(bf16[512,1024]{1,0:T(8,128)(2,1)} %tok_hbm.1, s32[1024,2048]{1,0:T(8,128)} %gate_hbm.1, s32[1024,2048]{1,0:T(8,128)} %up_hbm.1, s32[2048,1024]{1,0:T(8,128)} %down_hbm.1, s32[8,1,256]{2,1,0:T(1,128)} %bitcast.3, s32[8,1,256]{2,1,0:T(1,128)} %bitcast.4, s32[1,1024]{1,0:T(1,128)} %bitcast.5), custom_call_target="tpu_custom_call" | custom-call | flops 6442450944 | bytes 25165824 | tf_op jit(solution)/shard_map/pallas_call | solution.py:373
  78.0 1.5 %copy.9 = bf16[32,1024]{1,0:T(8,128)(2,1)} copy(bf16[32,1024]{1,0:T(8,128)(2,1)} %shard_map.73) | data formatting | bytes 131072

commit v2 on v1

--- a/solution.py
+++ b/solution.py
@@ -15,7 +15,7 @@
 OWN = TOKENS // (2 * NX)
 SUB = OWN // 2
 TILES = 8
-LAG_B, LAG_C, LAG_D = 1, 2, 3
+LAG_B, LAG_C, LAG_D = 1, 3, 6
 MESH = pl.DeviceIdType.MESH
 F32 = jnp.float32
 BF16 = jnp.bfloat16
@@ -63,7 +63,7 @@
     rot, z, a, r, y, part, gathered,
     tok_sem, code_sem, down_sem,
     core_ssem, core_rsem, x_ssem, x_rsem,
-    z_ssem, z_rsem, r_ssem, r_rsem, ag_ssem, ag_rsem, rs_ssem, rs_rsem,
+    z_ssem, z_rsem, r_ssem, r_rsem, ag_ssem, ag_rsem, rs_ssem, rs_rsem, plane_sem,
 ):
     dp = lax.axis_index("dp")
     me = lax.axis_index("tensor")
@@ -85,16 +85,6 @@
     def peer(k):
         return lax.rem(me + k, nt)
 
-    barrier = pltpu.get_barrier_semaphore()
-    for device in (dev_core, dev_right, dev_left):
-        pl.semaphore_signal(barrier, inc=1, device_id=device, device_id_type=MESH)
-
-    def greet(k, carry):
-        pl.semaphore_signal(barrier, inc=1, device_id=(dp, peer(k)), device_id_type=MESH)
-        return carry
-
-    lax.fori_loop(1, nt, greet, 0)
-
     tok_copy = pltpu.make_async_copy(tok_hbm, tok_in, tok_sem.at[0])
     tok_copy.start()
 
@@ -123,6 +113,15 @@
 
     lax.fori_loop(0, TILES, start_codes, 0)
     lax.fori_loop(0, TILES, start_down, 0)
+
+    barrier = pltpu.get_barrier_semaphore()
+    side = math.isqrt(nt)
+    row, col = me // side, me % side
+    along_y = [(dp, row * side + lax.rem(col + k, side)) for k in range(1, side)]
+    along_z = [(dp, lax.rem(row + k, side) * side + col) for k in range(1, side)]
+    greeted = [dev_core, dev_right, dev_left] + along_y + along_z
+    for device in greeted:
+        pl.semaphore_signal(barrier, inc=1, device_id=device, device_id_type=MESH)
 
     had[...] = signs(wide)
 
@@ -162,7 +161,9 @@
 
         @pl.when(t == 0)
         def _():
-            pl.semaphore_wait(barrier, 3 + nt - 1)
+            pl.semaphore_wait(barrier, len(greeted))
+            for device in along_z:
+                pl.semaphore_signal(plane_sem, inc=1, device_id=device, device_id_type=MESH)
 
         core_copy(t).start()
         acc[t] = jnp.dot(tok[own_rows, :], w[...], preferred_element_type=F32)
@@ -234,6 +235,7 @@
         z_copy(me, peer(k)).wait_recv()
         return carry
 
+    pl.semaphore_wait(plane_sem, len(along_z))
     lax.fori_loop(1, nt, z_send, 0)
     a[me] = z[me]
     lax.fori_loop(1, nt, z_wait, 0)
@@ -410,6 +412,7 @@
             dma((9,)),
             dma((NX, nt)),
             dma((NX, nt)),
+            pltpu.SemaphoreType.REGULAR,
         ],
         compiler_params=pltpu.CompilerParams(
             collective_id=0, has_side_effects=True, vmem_limit_bytes=56 * 1024 * 1024

time: 79.7 us -> 72.6 us (0.911)
  Pallas kernels: 78 us -> 70.9 us
    pallas_call x1, Pallas kernels: 78 us -> 70.9 us  [body(): pl.pallas_call(functools.partial(kernel, nt, units * nt), out_shape=jax.S...]
where the time goes in v2:
time: 72.6 us; the launch traced here: 72.4 us
  Pallas kernels  70.9 us (98%)
  local copies, waits for them, and re-layouts  1.47 us (2%)
    pallas_call x1, Pallas kernels, body(): pl.pallas_call(functools.partial(kernel, nt, units * nt), out_shape=jax.S...  70.9 us
    unnamed x1, local copies, waits for them, and re-layouts  1.47 us

profile of v2, /device:TPU:1, one launch (start us, length us, event | category | flops | bytes accessed | tf_op | source)
XLA Modules:
  0.0 72.4 jit_solution(551540909900265169)
XLA Ops:
  0.0 70.9 %shard_map.73 = bf16[32,1024]{1,0:T(8,128)(2,1)} custom-call(bf16[512,1024]{1,0:T(8,128)(2,1)} %tok_hbm.1, s32[1024,2048]{1,0:T(8,128)} %gate_hbm.1, s32[1024,2048]{1,0:T(8,128)} %up_hbm.1, s32[2048,1024]{1,0:T(8,128)} %down_hbm.1, s32[8,1,256]{2,1,0:T(1,128)} %bitcast.3, s32[8,1,256]{2,1,0:T(1,128)} %bitcast.4, s32[1,1024]{1,0:T(1,128)} %bitcast.5), custom_call_target="tpu_custom_call" | custom-call | flops 6442450944 | bytes 25165824 | tf_op jit(solution)/shard_map/pallas_call | solution.py:375
  70.9 1.5 %copy.9 = bf16[32,1024]{1,0:T(8,128)(2,1)} copy(bf16[32,1024]{1,0:T(8,128)(2,1)} %shard_map.73) | data formatting | bytes 131072

commit v3 on v0

v3 whole, which is shorter than its diff:
```python
import functools
import math

import jax
import jax.numpy as jnp
from jax import lax
from jax.experimental import pallas as pl
from jax.experimental.pallas import tpu as pltpu
from jax.sharding import PartitionSpec as P

D = 8192
FF = 32768
TOKENS = 512
NX = 4
OWN = TOKENS // (2 * NX)
CHUNKS = 2
PART = OWN // CHUNKS
TILES = 4
TURN = 256
UNITS = CHUNKS * TILES
UNITS = CHUNKS * TILES
MESH = pl.DeviceIdType.MESH
F32 = jnp.float32
BF16 = jnp.bfloat16


def remote(src, dst, send_sem, recv_sem, device):
    return pltpu.make_async_remote_copy(
        src_ref=src,
        dst_ref=dst,
        send_sem=send_sem,
        recv_sem=recv_sem,
        device_id=device,
        device_id_type=MESH,
    )


def walsh(parts):
    stride = 1
    while stride < len(parts):
        done = list(parts)
        for i in range(len(parts)):
            if i & stride == 0:
                done[i] = parts[i] + parts[i + stride]
                done[i + stride] = parts[i] - parts[i + stride]
        parts = done
        stride *= 2
    return parts


def signs(size):
    rows = lax.broadcasted_iota(jnp.int32, (size, size), 0)
    cols = lax.broadcasted_iota(jnp.int32, (size, size), 1)
    bits = jnp.bitwise_and(rows, cols)
    for shift in (8, 4, 2, 1):
        bits = jnp.bitwise_xor(bits, jnp.right_shift(bits, shift))
    return (1 - 2 * jnp.bitwise_and(bits, 1)).astype(F32).astype(BF16)


def kernel(
    nt, ff,
    tok_hbm, gate_hbm, up_hbm, down_hbm, gs_ref, us_ref, ds_ref,
    out_ref,
    tok_in, tok, codes, down_codes, wd, had,
    core_out, core_in, acc, x_out, x_in,
    z, a, r, y, part, gathered, final,
    tok_sem, code_sem, down_sem,
    core_ssem, core_rsem, x_ssem, x_rsem,
    z_ssem, z_rsem, r_ssem, r_rsem, ag_ssem, ag_rsem, rs_ssem, rs_rsem, plane_sem,
):
    dp = lax.axis_index("dp")
    me = lax.axis_index("tensor")
    x = dp // 2
    c = dp % 2
    right = lax.rem(x + 1, NX)
    left = lax.rem(x + NX - 1, NX)
    across = lax.rem(x + 2, NX)
    dev_core = (x * 2 + 1 - c, me)
    dev_right = (right * 2 + c, me)
    dev_left = (left * 2 + c, me)
    units = gate_hbm.shape[1]
    wide = units // TILES
    depth = gate_hbm.shape[0]
    group = TOKENS // (NX * nt * CHUNKS)
    piece = units // nt

    def peer(k):
        return lax.rem(me + k, nt)

    tok_copy = pltpu.make_async_copy(tok_hbm, tok_in, tok_sem.at[0])
    tok_copy.start()

    def code_copies(t):
        cols = pl.ds(t * wide, wide)
        return (
            pltpu.make_async_copy(gate_hbm.at[:, cols], codes.at[t, 0], code_sem.at[t, 0]),
            pltpu.make_async_copy(up_hbm.at[:, cols], codes.at[t, 1], code_sem.at[t, 1]),
        )

    def fetch(t):
        for copy in code_copies(t):
            copy.start()

    down_copy = pltpu.make_async_copy(down_hbm, down_codes, down_sem.at[0])
    fetch(0)

    barrier = pltpu.get_barrier_semaphore()
    side = math.isqrt(nt)
    row, col = me // side, me % side
    along_y = [(dp, row * side + lax.rem(col + k, side)) for k in range(1, side)]
    along_z = [(dp, lax.rem(row + k, side) * side + col) for k in range(1, side)]
    greeted = [dev_core, dev_right, dev_left] + along_y + along_z
    for device in greeted:
        pl.semaphore_signal(barrier, inc=1, device_id=device, device_id_type=MESH)

    tok_copy.wait()
    fetch(1)
    half_groups = nt // 2
    for half in range(2):
        for chip in range(NX):
            for q in range(CHUNKS):
                rows = []
                for j in range(half_groups):
                    first = (half * half_groups + j) * (TOKENS // nt) + (chip * CHUNKS + q) * group
                    span = max(16, group)
                    base = first // span * span
                    rows.append(tok_in[base : base + span, :].astype(F32)[first - base : first - base + group])
                start = lax.rem(half + c, 2) * (TOKENS // 2) + chip * OWN + q * PART
                tok[pl.ds(pl.multiple_of(start, PART), PART), :] = jnp.concatenate(rows, axis=0).astype(BF16)

    gate_cols = pl.ds(0, wide)
    up_cols = pl.ds(wide, wide)

    def core_copy(t):
        return remote(core_out.at[t], core_in.at[t], core_ssem.at[t], core_rsem.at[t], dev_core)

    def x_copy(u, way, kind):
        return remote(
            x_out.at[u, way, kind], x_in.at[u, way, kind], x_ssem.at[u, way, kind], x_rsem.at[u, way, kind],
            dev_right if way == 0 else dev_left,
        )

    def multiply(t):
        for copy in code_copies(t):
            copy.wait()
        if t + 2 < TILES:
            fetch(t + 2)
        elif t + 2 == TILES:
            down_copy.start()
        for side, cols in ((0, gate_cols), (1, up_cols)):
            weights = (codes[t, side] - 8).astype(F32).astype(BF16)
            product = jnp.dot(tok[...], weights, preferred_element_type=F32)
            acc[t, :, cols] = product[: TOKENS // 2]
            core_out[t, :, cols] = product[TOKENS // 2 :].astype(BF16)
        if t == 0:
            pl.semaphore_wait(barrier, len(greeted))
        core_copy(t).start()

    def convert_down(t):
        rows = pl.ds(t * (units // TILES), units // TILES)
        wd[rows, :] = (down_codes[rows, :] - 8).astype(F32).astype(BF16)

    def unit_rows(u, chip):
        return pl.ds(pl.multiple_of(chip * OWN + u // TILES * PART, PART), PART)

    def both(u, chip, cols):
        rows = unit_rows(u, chip)
        return acc[u % TILES, rows, cols] + core_in[u % TILES, rows, cols].astype(F32)

    def stage_b(u):
        if u < TILES:
            core_copy(u).wait()
        for kind, pieces in ((0, ((across, gate_cols), (across, up_cols))), (1, ((right, up_cols), (left, gate_cols)))):
            for way in range(2):
                x_out[u, way, kind] = both(u, *pieces[way]).astype(BF16)
                x_copy(u, way, kind).start()

    def stage_c(u):
        for way, (chip, cols) in enumerate(((right, gate_cols), (left, up_cols))):
            x_copy(u, way, 0).wait_recv()
            x_out[u, way, 2] = (both(u, chip, cols) + x_in[u, way, 0].astype(F32)).astype(BF16)
            x_copy(u, way, 2).start()

    def stage_d(q):
        unit = 1.0 / (128.0 * math.sqrt(D))
        stacked = []
        for u in range(q * TILES, (q + 1) * TILES):
            t = u % TILES
            for way in range(2):
                for kind in (1, 2):
                    x_copy(u, way, kind).wait_recv()
            gate = both(u, x, gate_cols) + x_in[u, 0, 2].astype(F32) + x_in[u, 1, 1].astype(F32)
            gate = gate * (gs_ref[t].astype(F32) * unit)
            up = both(u, x, up_cols) + x_in[u, 0, 1].astype(F32) + x_in[u, 1, 2].astype(F32)
            up = up * (us_ref[t].astype(F32) * unit)
            hidden = gate / (1.0 + jnp.exp(-gate)) * up
            for col in range(0, wide, TURN):
                stacked.append(hidden[:, col : col + TURN].astype(BF16))
        turned = jnp.dot(jnp.concatenate(stacked, axis=0), had[...], preferred_element_type=F32)
        mixed = walsh([turned[i * PART : (i + 1) * PART] for i in range(len(stacked))])
        flat = jnp.concatenate(mixed, axis=1).astype(BF16)
        for j in range(nt):
            z[q, j] = flat[:, j * piece : (j + 1) * piece]

    def z_copy(q, j, slot):
        return remote(z.at[q, j], a.at[q, slot], z_ssem.at[q, j], z_rsem.at[q, slot], (dp, j))

    def stage_e(q):
        if q == 0:
            pl.semaphore_wait(plane_sem, len(along_z))

        def send(k, carry):
            z_copy(q, peer(k), me).start()
            return carry

        lax.fori_loop(1, nt, send, 0)
        a[q, me] = z[q, me]

    def chunk_rows(core):
        return pl.ds(pl.multiple_of(core * PART, PART), PART)

    def r_copy(q, j, slot):
        cols = pl.ds(pl.multiple_of(slot * piece, piece), piece)
        return remote(r.at[q, j], y.at[q, x, chunk_rows(c), cols], r_ssem.at[q, j], r_rsem.at[q, slot], (dp, j))

    def stage_f(q):
        def wait(k, carry):
            z_copy(q, me, peer(k)).wait_recv()
            return carry

        lax.fori_loop(1, nt, wait, 0)
        for rows in range(0, PART, 16):
            mixed = walsh([a[q, i, rows : rows + 16, :].astype(F32) for i in range(nt)])
            for j in range(nt):
                r[q, j, rows : rows + 16, :] = (mixed[j] * (1.0 / math.sqrt(ff))).astype(BF16)

        def send(k, carry):
            r_copy(q, peer(k), me).start()
            return carry

        lax.fori_loop(1, nt, send, 0)
        y[q, x, chunk_rows(c), pl.ds(pl.multiple_of(me * piece, piece), piece)] = r[q, me]

        def sent(k, carry):
            z_copy(q, peer(k), me).wait_send()
            return carry

        lax.fori_loop(1, nt, sent, 0)

    def gather(q, n, core=None):
        core = c if core is None else core
        low = pl.ds(pl.multiple_of(core * PART, PART // 2), PART // 2)
        high = pl.ds(pl.multiple_of(core * PART + PART // 2, PART // 2), PART // 2)
        whole = chunk_rows(core)
        chip, rows, device = (
            (x, low, dev_right), (x, high, dev_right), (x, high, dev_left), (x, low, dev_left), (x, whole, dev_core),
            (left, low, dev_right), (right, high, dev_left),
            (left, whole, dev_core), (right, whole, dev_core), (across, low, dev_core), (across, high, dev_core),
        )[n]
        block = y.at[q, chip, rows, :]
        return remote(block, block, ag_ssem.at[q, n], ag_rsem.at[q, n], device)

    def arrived(q, n):
        low = pl.ds(pl.multiple_of(c * PART, PART // 2), PART // 2)
        high = pl.ds(pl.multiple_of(c * PART + PART // 2, PART // 2), PART // 2)
        places = {
            0: (left, low), 1: (left, high), 2: (right, high), 3: (right, low), 5: (across, low), 6: (across, high),
        }
        if n in places:
            chip, rows = places[n]
            block = y.at[q, chip, rows, :]
            remote(block, block, ag_ssem.at[q, n], ag_rsem.at[q, n], dev_core).wait_recv()
        else:
            gather(q, n, 1 - c).wait_recv()

    def gather_start(q):
        def wait(k, carry):
            r_copy(q, me, peer(k)).wait_recv()
            return carry

        lax.fori_loop(1, nt, wait, 0)
        for n in (0, 2, 1, 3, 4):
            gather(q, n).start()

    def gather_on(q, pairs):
        for come, go in pairs:
            arrived(q, come)
            if go is not None:
                gather(q, go).start()

    def rs_copy(q, pair, j, slot):
        return remote(
            part.at[q, pair, j], gathered.at[q, pair, slot], rs_ssem.at[q, pair, j], rs_rsem.at[q, pair, slot], (dp, j)
        )

    def down(q, pair):
        first, second = ((x, left), (right, across))[pair]
        rows_in = jnp.concatenate([y[q, first], y[q, second]], axis=0)
        result = jnp.dot(rows_in, wd[...], preferred_element_type=F32)
        middle = result.shape[1] // 2
        for j in range(nt):
            rows = jnp.concatenate(
                [result[j * group : (j + 1) * group], result[(nt + j) * group : (nt + j + 1) * group]], axis=0
            )
            part[q, pair, j] = jnp.concatenate([rows[:, :middle], rows[:, middle:]], axis=0).astype(BF16)

        def send(k, carry):
            rs_copy(q, pair, peer(k), me).start()
            return carry

        lax.fori_loop(1, nt, send, 0)
        gathered[q, pair, me] = part[q, pair, me]

    def total(q, pair):
        def wait(k, carry):
            rs_copy(q, pair, me, peer(k)).wait_recv()
            return carry

        lax.fori_loop(1, nt, wait, 0)
        both = gathered[q, pair, 0].astype(F32)
        for i in range(1, nt):
            both = both + gathered[q, pair, i].astype(F32)
        rows = jnp.concatenate([both[: 2 * group], both[2 * group :]], axis=1)
        first, second = ((x, left), (right, across))[pair]
        final[first, q] = rows[:group]
        final[second, q] = rows[group:]

    multiply(0)
    for device in along_z:
        pl.semaphore_signal(plane_sem, inc=1, device_id=device, device_id_type=MESH)
    multiply(1)
    stage_b(0)
    multiply(2)
    stage_b(1)
    multiply(3)
    stage_b(2)
    stage_c(0)
    had[...] = signs(TURN)
    stage_b(3)
    stage_c(1)
    down_copy.wait()
    convert_down(0)
    stage_c(2)
    convert_down(1)
    stage_c(3)
    for u in range(TILES, UNITS):
        stage_b(u)
    convert_down(2)
    convert_down(3)
    stage_d(0)
    stage_e(0)
    stage_c(4)
    stage_c(5)
    stage_c(6)
    stage_f(0)
    stage_c(7)
    stage_d(1)
    stage_e(1)
    gather_start(0)
    gather_on(0, ((0, 5), (2, 6)))
    stage_f(1)
    gather_on(0, ((1, 7), (3, 8), (4, None), (7, None)))
    down(0, 0)
    gather_on(0, ((5, 9), (6, 10), (8, None), (9, None), (10, None)))
    down(0, 1)
    gather_start(1)
    gather_on(1, ((0, 5), (2, 6)))
    total(0, 0)
    gather_on(1, ((1, 7), (3, 8), (4, None), (7, None)))
    down(1, 0)
    gather_on(1, ((5, 9), (6, 10), (8, None), (9, None), (10, None)))
    down(1, 1)

    def peers_sent(k, carry):
        for q in range(CHUNKS):
            r_copy(q, peer(k), me).wait_send()
            for pair in range(2):
                rs_copy(q, pair, peer(k), me).wait_send()
        return carry

    lax.fori_loop(1, nt, peers_sent, 0)
    for q in range(CHUNKS):
        for n in range(11):
            gather(q, n).wait_send()
    for u in range(UNITS):
        for way in range(2):
            for kind in range(3):
                x_copy(u, way, kind).wait_send()

    total(0, 1)
    total(1, 0)
    total(1, 1)
    scale = ds_ref[...].astype(F32) * (1.0 / (64.0 * math.sqrt(ff)))
    blocks = [final[chip, q] for chip in range(NX) for q in range(CHUNKS)]
    out_ref[...] = (jnp.concatenate(blocks, axis=0) * scale).astype(BF16)


def body(tokens, gate_codes, up_codes, down_codes, gate_scale, up_scale, down_scale):
    nt = lax.axis_size("tensor")
    depth, units = gate_codes.shape
    width = down_codes.shape[1]
    wide = units // TILES
    piece = units // nt
    group = TOKENS // (NX * nt * CHUNKS)
    dma = pltpu.SemaphoreType.DMA
    any_space = pl.BlockSpec(memory_space=pl.ANY)
    vmem = pl.BlockSpec(memory_space=pltpu.VMEM)
    return pl.pallas_call(
        functools.partial(kernel, nt, units * nt),
        out_shape=jax.ShapeDtypeStruct((TOKENS // nt, width), BF16),
        in_specs=[any_space] * 4 + [vmem] * 3,
        out_specs=vmem,
        scratch_shapes=[
            pltpu.VMEM((TOKENS, depth), BF16),
            pltpu.VMEM((TOKENS, depth), BF16),
            pltpu.VMEM((TILES, 2, depth, wide), jnp.int32),
            pltpu.VMEM((units, width), jnp.int32),
            pltpu.VMEM((units, width), BF16),
            pltpu.VMEM((TURN, TURN), BF16),
            pltpu.VMEM((TILES, TOKENS // 2, 2 * wide), BF16),
            pltpu.VMEM((TILES, TOKENS // 2, 2 * wide), BF16),
            pltpu.VMEM((TILES, TOKENS // 2, 2 * wide), F32),
            pltpu.VMEM((UNITS, 2, 3, PART, wide), BF16),
            pltpu.VMEM((UNITS, 2, 3, PART, wide), BF16),
            pltpu.VMEM((CHUNKS, nt, PART, piece), BF16),
            pltpu.VMEM((CHUNKS, nt, PART, piece), BF16),
            pltpu.VMEM((CHUNKS, nt, PART, piece), BF16),
            pltpu.VMEM((CHUNKS, NX, 2 * PART, units), BF16),
            pltpu.VMEM((CHUNKS, 2, nt, 4 * group, width // 2), BF16),
            pltpu.VMEM((CHUNKS, 2, nt, 4 * group, width // 2), BF16),
            pltpu.VMEM((NX, CHUNKS, group, width), F32),
            dma((1,)),
            dma((TILES, 2)),
            dma((1,)),
            dma((TILES,)),
            dma((TILES,)),
            dma((UNITS, 2, 3)),
            dma((UNITS, 2, 3)),
            dma((CHUNKS, nt)),
            dma((CHUNKS, nt)),
            dma((CHUNKS, nt)),
            dma((CHUNKS, nt)),
            dma((CHUNKS, 11)),
            dma((CHUNKS, 11)),
            dma((CHUNKS, 2, nt)),
            dma((CHUNKS, 2, nt)),
            pltpu.SemaphoreType.REGULAR,
        ],
        compiler_params=pltpu.CompilerParams(
            collective_id=0, has_side_effects=True, vmem_limit_bytes=56 * 1024 * 1024
        ),
        cost_estimate=pl.CostEstimate(
            flops=2 * TOKENS * depth * 3 * units, bytes_accessed=12 * depth * units, transcendentals=OWN * units
        ),
    )(
        tokens, gate_codes, up_codes, down_codes,
        gate_scale.reshape(TILES, 1, wide), up_scale.reshape(TILES, 1, wide), down_scale.reshape(1, width),
    )


def solution(mesh):
    in_specs = (
        P(None, "dp"),
        P("dp", "tensor"),
        P("dp", "tensor"),
        P("tensor", "dp"),
        P("tensor"),
        P("tensor"),
        P("dp"),
    )
    return jax.shard_map(body, mesh=mesh, in_specs=in_specs, out_specs=P("tensor", "dp"), check_vma=False)
```

time: 230 us -> 65.9 us (0.29)
  waiting for transfers between devices: 163 us -> 0 us
  Pallas kernels: 0 us -> 64.3 us
  matrix products: 21.9 us -> 0 us
  other arithmetic: 14.5 us -> 0 us
  between operations: 13.2 us -> 0.01 us
  starting transfers between devices: 8.56 us -> 0 us
  local copies, waits for them, and re-layouts: 8.05 us -> 1.47 us
    reduce_scatter x1 -> x0, waiting for transfers between devices: 71.6 us -> none  [body(): lax.psum_scatter(partial_value.astype(jnp.bfloat16), 'tensor', scatter_di...]
    pallas_call x0 -> x1, Pallas kernels: none -> 64.3 us  [body(): pl.pallas_call(functools.partial(kernel, nt, units * nt), out_shape=jax.S...]
    unnamed x4 -> x0, waiting for transfers between devices: 38.2 us -> none
    all_gather x1 -> x0, waiting for transfers between devices: 32.7 us -> none  [body(): lax.all_gather(rotated, 'dp', axis=0, tiled=True)]
    dot_general x3 -> x0, matrix products: 21.9 us -> none  [the longest x1 10 us: body(): jnp.dot(tokens, paired, preferred_element_type=jnp.float32)]
    ppermute x4 -> x0, waiting for transfers between devices: 20.6 us -> none  [partner_2(): return lax.ppermute(value, axis, pairs)]
    convert_element_type x7 -> x0, other arithmetic: 14.5 us -> none  [the longest x1 11.7 us: body(): (up_codes - 8).astype(jnp.bfloat16)]
    ppermute x4 -> x0, starting transfers between devices: 8.47 us -> none  [partner_2(): return lax.ppermute(value, axis, pairs)]
  transfers between devices with their start and end apart: 7 -> 0, of which waited for: 7 -> 0; matrix products, arithmetic and copies ran while one was open for 0% -> 0% of each run, Pallas kernels for 0% -> 0%
where the time goes in v3:
time: 65.9 us; the launch traced here: 65.7 us
  Pallas kernels  64.3 us (98%)
  local copies, waits for them, and re-layouts  1.47 us (2%)
    pallas_call x1, Pallas kernels, body(): pl.pallas_call(functools.partial(kernel, nt, units * nt), out_shape=jax.S...  64.3 us
    unnamed x1, local copies, waits for them, and re-layouts  1.47 us

profile of v3, /device:TPU:1, one launch (start us, length us, event | category | flops | bytes accessed | tf_op | source)
XLA Modules:
  0.0 65.7 jit_solution(2303879002436973688)
XLA Ops:
  0.0 64.3 %shard_map.73 = bf16[32,1024]{1,0:T(8,128)(2,1)} custom-call(bf16[512,1024]{1,0:T(8,128)(2,1)} %tok_hbm.1, s32[1024,2048]{1,0:T(8,128)} %gate_hbm.1, s32[1024,2048]{1,0:T(8,128)} %up_hbm.1, s32[2048,1024]{1,0:T(8,128)} %down_hbm.1, s32[4,1,512]{2,1,0:T(1,128)} %bitcast.3, s32[4,1,512]{2,1,0:T(1,128)} %bitcast.4, s32[1,1024]{1,0:T(1,128)} %bitcast.5), custom_call_target="tpu_custom_call" | custom-call | flops 6442450944 | bytes 25165824 | tf_op jit(solution)/shard_map/pallas_call | solution.py:408
  64.3 1.5 %copy.9 = bf16[32,1024]{1,0:T(8,128)(2,1)} copy(bf16[32,1024]{1,0:T(8,128)(2,1)} %shard_map.73) | data formatting | bytes 131072

commit v4 on v3

--- a/solution.py
+++ b/solution.py
@@ -33,6 +33,12 @@
         device_id=device,
         device_id_type=MESH,
     )
+
+
+def unrolled(low, high, step, carry):
+    for k in range(low, high):
+        carry = step(k, carry)
+    return carry
 
 
 def walsh(parts):
@@ -145,7 +151,7 @@
             copy.wait()
         if t + 2 < TILES:
             fetch(t + 2)
-        elif t + 2 == TILES:
+        elif t + 1 == TILES:
             down_copy.start()
         for side, cols in ((0, gate_cols), (1, up_cols)):
             weights = (codes[t, side] - 8).astype(F32).astype(BF16)
@@ -213,7 +219,7 @@
             z_copy(q, peer(k), me).start()
             return carry
 
-        lax.fori_loop(1, nt, send, 0)
+        unrolled(1, nt, send, 0)
         a[q, me] = z[q, me]
 
     def chunk_rows(core):
@@ -228,7 +234,7 @@
             z_copy(q, me, peer(k)).wait_recv()
             return carry
 
-        lax.fori_loop(1, nt, wait, 0)
+        unrolled(1, nt, wait, 0)
         for rows in range(0, PART, 16):
             mixed = walsh([a[q, i, rows : rows + 16, :].astype(F32) for i in range(nt)])
             for j in range(nt):
@@ -238,14 +244,14 @@
             r_copy(q, peer(k), me).start()
             return carry
 
-        lax.fori_loop(1, nt, send, 0)
+        unrolled(1, nt, send, 0)
         y[q, x, chunk_rows(c), pl.ds(pl.multiple_of(me * piece, piece), piece)] = r[q, me]
 
         def sent(k, carry):
             z_copy(q, peer(k), me).wait_send()
             return carry
 
-        lax.fori_loop(1, nt, sent, 0)
+        unrolled(1, nt, sent, 0)
 
     def gather(q, n, core=None):
         core = c if core is None else core
@@ -278,7 +284,7 @@
             r_copy(q, me, peer(k)).wait_recv()
             return carry
 
-        lax.fori_loop(1, nt, wait, 0)
+        unrolled(1, nt, wait, 0)
         for n in (0, 2, 1, 3, 4):
             gather(q, n).start()
 
@@ -308,7 +314,7 @@
             rs_copy(q, pair, peer(k), me).start()
             return carry
 
-        lax.fori_loop(1, nt, send, 0)
+        unrolled(1, nt, send, 0)
         gathered[q, pair, me] = part[q, pair, me]
 
     def total(q, pair):
@@ -316,7 +322,7 @@
             rs_copy(q, pair, me, peer(k)).wait_recv()
             return carry
 
-        lax.fori_loop(1, nt, wait, 0)
+        unrolled(1, nt, wait, 0)
         both = gathered[q, pair, 0].astype(F32)
         for i in range(1, nt):
             both = both + gathered[q, pair, i].astype(F32)
@@ -335,39 +341,37 @@
     multiply(3)
     stage_b(2)
     stage_c(0)
-    had[...] = signs(TURN)
     stage_b(3)
     stage_c(1)
-    down_copy.wait()
-    convert_down(0)
+    had[...] = signs(TURN)
     stage_c(2)
-    convert_down(1)
     stage_c(3)
     for u in range(TILES, UNITS):
         stage_b(u)
-    convert_down(2)
-    convert_down(3)
     stage_d(0)
     stage_e(0)
     stage_c(4)
+    down_copy.wait()
+    convert_down(0)
     stage_c(5)
+    convert_down(1)
     stage_c(6)
+    convert_down(2)
+    convert_down(3)
     stage_f(0)
     stage_c(7)
     stage_d(1)
     stage_e(1)
     gather_start(0)
-    gather_on(0, ((0, 5), (2, 6)))
     stage_f(1)
-    gather_on(0, ((1, 7), (3, 8), (4, None), (7, None)))
+    gather_on(0, ((0, 5), (2, 6), (1, 7), (3, 8), (4, None), (7, None)))
     down(0, 0)
+    gather_start(1)
     gather_on(0, ((5, 9), (6, 10), (8, None), (9, None), (10, None)))
     down(0, 1)
-    gather_start(1)
-    gather_on(1, ((0, 5), (2, 6)))
+    gather_on(1, ((0, 5), (2, 6), (1, 7), (3, 8), (4, None), (7, None)))
+    down(1, 0)
     total(0, 0)
-    gather_on(1, ((1, 7), (3, 8), (4, None), (7, None)))
-    down(1, 0)
     gather_on(1, ((5, 9), (6, 10), (8, None), (9, None), (10, None)))
     down(1, 1)
 
@@ -378,7 +382,7 @@
                 rs_copy(q, pair, peer(k), me).wait_send()
         return carry
 
-    lax.fori_loop(1, nt, peers_sent, 0)
+    unrolled(1, nt, peers_sent, 0)
     for q in range(CHUNKS):
         for n in range(11):
             gather(q, n).wait_send()

time: 65.9 us -> 63.7 us (0.967)
  Pallas kernels: 64.3 us -> 62.1 us
    pallas_call x1, Pallas kernels: 64.3 us -> 62.1 us  [body(): pl.pallas_call(functools.partial(kernel, nt, units * nt), out_shape=jax.S...]
where the time goes in v4:
time: 63.7 us; the launch traced here: 63.6 us
  Pallas kernels  62.1 us (97%)
  local copies, waits for them, and re-layouts  1.47 us (2%)
    pallas_call x1, Pallas kernels, body(): pl.pallas_call(functools.partial(kernel, nt, units * nt), out_shape=jax.S...  62.1 us
    unnamed x1, local copies, waits for them, and re-layouts  1.47 us

profile of v4, /device:TPU:1, one launch (start us, length us, event | category | flops | bytes accessed | tf_op | source)
XLA Modules:
  0.0 63.6 jit_solution(986006560913696204)
XLA Ops:
  0.0 62.1 %shard_map.73 = bf16[32,1024]{1,0:T(8,128)(2,1)} custom-call(bf16[512,1024]{1,0:T(8,128)(2,1)} %tok_hbm.1, s32[1024,2048]{1,0:T(8,128)} %gate_hbm.1, s32[1024,2048]{1,0:T(8,128)} %up_hbm.1, s32[2048,1024]{1,0:T(8,128)} %down_hbm.1, s32[4,1,512]{2,1,0:T(1,128)} %bitcast.3, s32[4,1,512]{2,1,0:T(1,128)} %bitcast.4, s32[1,1024]{1,0:T(1,128)} %bitcast.5), custom_call_target="tpu_custom_call" | custom-call | flops 6442450944 | bytes 25165824 | tf_op jit(solution)/shard_map/pallas_call | solution.py:412
  62.1 1.5 %copy.9 = bf16[32,1024]{1,0:T(8,128)(2,1)} copy(bf16[32,1024]{1,0:T(8,128)(2,1)} %shard_map.73) | data formatting | bytes 131072

commit v5 on v4

--- a/solution.py
+++ b/solution.py
@@ -358,8 +358,8 @@
     stage_c(6)
     convert_down(2)
     convert_down(3)
+    stage_c(7)
     stage_f(0)
-    stage_c(7)
     stage_d(1)
     stage_e(1)
     gather_start(0)

time: 63.7 us -> 63.2 us (level)
  no operation moved by 1% of the time
where the time goes in v5:
time: 63.2 us; the launch traced here: 63 us
  Pallas kernels  61.5 us (97%)
  local copies, waits for them, and re-layouts  1.47 us (2%)
    pallas_call x1, Pallas kernels, body(): pl.pallas_call(functools.partial(kernel, nt, units * nt), out_shape=jax.S...  61.5 us
    unnamed x1, local copies, waits for them, and re-layouts  1.47 us

profile of v5, /device:TPU:1, one launch (start us, length us, event | category | flops | bytes accessed | tf_op | source)
XLA Modules:
  0.0 63.0 jit_solution(9126339949179275927)
XLA Ops:
  0.0 61.5 %shard_map.73 = bf16[32,1024]{1,0:T(8,128)(2,1)} custom-call(bf16[512,1024]{1,0:T(8,128)(2,1)} %tok_hbm.1, s32[1024,2048]{1,0:T(8,128)} %gate_hbm.1, s32[1024,2048]{1,0:T(8,128)} %up_hbm.1, s32[2048,1024]{1,0:T(8,128)} %down_hbm.1, s32[4,1,512]{2,1,0:T(1,128)} %bitcast.3, s32[4,1,512]{2,1,0:T(1,128)} %bitcast.4, s32[1,1024]{1,0:T(1,128)} %bitcast.5), custom_call_target="tpu_custom_call" | custom-call | flops 6442450944 | bytes 25165824 | tf_op jit(solution)/shard_map/pallas_call | solution.py:412
  61.5 1.5 %copy.9 = bf16[32,1024]{1,0:T(8,128)(2,1)} copy(bf16[32,1024]{1,0:T(8,128)(2,1)} %shard_map.73) | data formatting | bytes 131072
